TPU v7x, 512 devices: a whole 4x8x8 slice. The times are simulated.
512 devices in a mesh: grp: 32 (over x, z), tp: 16 (over y, core).
Axes of the slice: x: 4, y: 8, z: 8, core: 2. Of those that a mesh axis runs over, the one named last changes fastest.
Arguments:
- acts: bfloat16 [4096, 8192], P('grp', 'tp'), may hold values from -6 to 6
- grads: bfloat16 [4096, 4096], P('grp'), may hold values from -1.5 to 1.5
- counts: int32 [32, 24], P('grp'), may hold values from 1 to 12, 128 in all within a row
- owner_slot: int32 [24], replicated, may hold values from 0 to 31, as said below
- base_weight: bfloat16 [8192, 4096], P('tp', 'grp')
- adapter_a: bfloat16 [32, 8192, 32], P('grp', 'tp'), may hold values from -0.0625 to 0.0625
- adapter_b: bfloat16 [32, 32, 4096], P('grp'), may hold values from -0.59765625 to 0.59765625
- magnitude: float32 [32, 4096], P('grp'), may hold values from 0.5 to 2
Outputs:
- row_grad: bfloat16 [4096, 8192], P('grp', 'tp')
- grad_a: float32 [32, 8192, 32], P('grp', 'tp')
- grad_b: float32 [32, 32, 4096], P('grp', None, 'tp')
- grad_gain: float32 [32, 4096], P('grp')
Inputs may be any that keep to these rules, and one draw needn't show every extreme that they name: Every tenant has one row or more on every index of grp; the largest count in each row of counts is exactly 12. `owner_slot`: distinct slots, one for each tenant; slot p lies on index p // 1 of grp; other slots are unused.
All inputs are finite; a program needn't handle non-finite values.
Results may differ from a plain program's by a relative error of at most 0.0095.
Values may be sent and summed in bfloat16 or wider, within the bound.
No kernel may reach another device: no remote copies, remote signals or barrier semaphores. Data moves between devices by JAX's collectives and lax.ppermute only.
A program may use at most 64 MiB of HBM per device.

v0:
```python
import jax
import jax.numpy as jnp
from jax import lax
from jax.sharding import PartitionSpec as P

CAP = 12
NX = 4
EPSILON = 1e-06
HIGH = lax.Precision.HIGHEST
BF = jnp.bfloat16
F32 = jnp.float32


def dot(left, right, dims, precision=None):
    return lax.dot_general(
        left, right, (dims, ((), ())), precision=precision, preferred_element_type=F32
    )


def split_pair(values):
    upper = values.astype(BF)
    return (upper, (values - upper.astype(F32)).astype(BF))


def row_targets(count_row, owner_slot, rows):
    ends = jnp.cumsum(count_row)
    starts = ends - count_row
    ids = jnp.arange(rows, dtype=jnp.int32)[None, :]
    inside = ((ids >= starts[:, None]) & (ids < ends[:, None])).astype(jnp.int32)
    shift = owner_slot * CAP - starts
    return jnp.sum(inside * shift[:, None], axis=0) + ids[0]


def on_device(acts, grads, counts, owner_slot, base_weight, adapter_a, adapter_b, magnitude):
    groups, shards = (lax.axis_size("grp"), lax.axis_size("tp"))
    nz = groups // NX
    quads = shards // NX
    rows, width = acts.shape
    out_width = grads.shape[1]
    rank = adapter_a.shape[2]
    x_cols, t_cols = (out_width // NX, out_width // shards)
    packed = groups * CAP
    z_groups = [[i * nz + j for j in range(nz)] for i in range(NX)]
    x_groups = [[i * nz + j for i in range(NX)] for j in range(nz)]
    my_x = lax.axis_index("grp") // nz
    my_t = lax.axis_index("tp")
    weight_x = lax.all_gather(base_weight.T, "grp", axis=0, tiled=True, axis_index_groups=z_groups)
    target = row_targets(counts[0], owner_slot, rows)
    place = (jnp.arange(packed, dtype=jnp.int32)[:, None] == target[None, :]).astype(BF)
    grads_t = lax.dynamic_slice(grads, (0, my_t * t_cols), (rows, t_cols))
    both = dot(place, jnp.concatenate([acts, grads_t], axis=1), ((1,), (0,))).astype(BF)
    both = lax.all_to_all(
        both.reshape(groups, CAP, width + t_cols), "grp", split_axis=0, concat_axis=0, tiled=True
    ).reshape(packed, width + t_cols)
    rows_in, rows_grad_t = (both[:, :width], both[:, width:])
    rows_grad = lax.all_gather(rows_grad_t, "tp", axis=1, tiled=True)
    first, second = (adapter_a[0], adapter_b[0])
    first_t = first.T
    fields = jnp.concatenate(
        [
            jnp.broadcast_to(first_t[None], (NX, rank, width)),
            second.reshape(rank, NX, x_cols).transpose(1, 0, 2),
        ],
        axis=2,
    )
    fields = lax.all_to_all(
        fields, "grp", split_axis=0, concat_axis=0, tiled=True, axis_index_groups=x_groups
    ).reshape(NX * rank, width + x_cols)
    first_all, second_all = (fields[:, :width], fields[:, width:])
    second_wide = second_all.astype(F32)
    owner = jnp.arange(NX * rank, dtype=jnp.int32) // rank
    gram = jnp.where(owner[:, None] == owner[None, :], dot(first_all, first_all, ((1,), (1,))), 0.0)
    gram_second = dot(gram, second_wide, ((1,), (0,)), HIGH)
    first_weight = dot(first_all, weight_x, ((1,), (1,)))
    square_base = jnp.sum(jnp.square(weight_x.astype(F32)), axis=1)
    squares = square_base[None, :] + jnp.sum(
        (second_wide * (2.0 * first_weight + gram_second)).reshape(NX, rank, x_cols), axis=1
    )
    first_merged = first_weight + gram_second
    rows_low = dot(first_t, rows_in, ((1,), (1,)))

    def lanes(values):
        return jnp.concatenate(
            [values[:, i : i + 128] for i in range(0, values.shape[1], 128)], axis=0
        )

    pieces = first_merged.astype(BF).reshape(NX, rank, quads, t_cols)
    pieces = pieces.transpose(0, 2, 1, 3).reshape(shards, rank, t_cols)
    pieces = jnp.concatenate([pieces[:, :, i : i + 128] for i in range(0, t_cols, 128)], axis=1)
    square_upper, square_lower = split_pair(squares)
    common = jnp.concatenate(
        [lanes(square_upper), lanes(square_lower), lanes(rows_low.astype(BF))], axis=0
    )
    sums = jnp.concatenate(
        [pieces, jnp.broadcast_to(common[None], (shards,) + common.shape)], axis=1
    )
    sums = lax.all_to_all(sums, "tp", split_axis=0, concat_axis=0, tiled=True)
    sums = jnp.sum(sums.astype(F32), axis=0)

    def unlanes(values, height):
        return jnp.concatenate(
            [values[i : i + height] for i in range(0, values.shape[0], height)], axis=1
        )

    n_piece = rank * t_cols // 128
    n_square = NX * x_cols // 128
    merged_piece = unlanes(sums[:n_piece], rank)
    square_sum = unlanes(
        sums[n_piece : n_piece + n_square] + sums[n_piece + n_square : n_piece + 2 * n_square], NX
    )
    rows_low = unlanes(sums[n_piece + 2 * n_square :], rank)
    square_own = lax.all_to_all(
        square_sum.reshape(NX, 1, x_cols),
        "grp",
        split_axis=0,
        concat_axis=0,
        tiled=True,
        axis_index_groups=x_groups,
    ).reshape(1, out_width)
    swap = []
    for i in range(NX):
        for j in range(nz):
            for a in range(NX):
                for q in range(quads):
                    swap.append(
                        (
                            (i * nz + j) * shards + a * quads + q,
                            (a * nz + j) * shards + i * quads + q,
                        )
                    )
    merged_own = lax.ppermute(merged_piece, ("grp", "tp"), swap)
    norm = jnp.sqrt(square_own + EPSILON)
    scale = magnitude / norm

    def along_x(values, step):
        pairs = [((i + step) % NX * nz + j, i * nz + j) for i in range(NX) for j in range(nz)]
        return lax.ppermute(values, "grp", pairs)

    after = along_x(weight_x, 1)
    before = along_x(weight_x, -1)
    half = x_cols // 2
    across = jnp.concatenate([along_x(after[:half], 1), along_x(before[half:], -1)], axis=0)
    weight = jnp.zeros((out_width, width), BF)
    for piece, step in ((weight_x, 0), (after, 1), (across, 2), (before, 3)):
        weight = lax.dynamic_update_slice(weight, piece, ((my_x + step) % NX * x_cols, 0))
    hidden = (rows_grad.astype(F32) * scale).astype(BF)
    inner = dot(hidden, second, ((1,), (1,))).astype(BF)
    back = dot(hidden, weight, ((1,), (0,))) + dot(inner, first, ((1,), (1,)))
    back = lax.all_to_all(
        back.astype(BF).reshape(groups, CAP, width), "grp", split_axis=0, concat_axis=0, tiled=True
    ).reshape(packed, width)
    row_grad = dot(place, back, ((0,), (0,))).astype(BF)
    projected = dot(rows_in, weight, ((1,), (1,)))
    align = jnp.sum(rows_grad.astype(F32) * projected, axis=0)
    second_t = lax.dynamic_slice(second, (0, my_t * t_cols), (rank, t_cols)).astype(F32)
    first_moment = dot(rows_low.astype(BF), rows_grad_t, ((1,), (0,)))
    align_low = jnp.sum(first_moment * second_t, axis=0)
    align_t = lax.dynamic_slice(align, (my_t * t_cols,), (t_cols,)) + align_low
    align = lax.dynamic_update_slice(align, align_t, (my_t * t_cols,))
    align_all = lax.all_to_all(
        jnp.broadcast_to(align.reshape(1, -1, 128), (shards, out_width // 128, 128)),
        "tp",
        split_axis=0,
        concat_axis=0,
        tiled=True,
    )
    align = jnp.sum(align_all, axis=0).reshape(1, out_width)
    grad_gain = align / norm
    shrink = magnitude * align / (norm * norm * norm)
    shrunk = (second.astype(F32) * shrink).astype(BF)
    small = dot(second, shrunk, ((1,), (1,)))
    grad_a = (
        dot(rows_in, inner, ((0,), (0,)))
        - dot(weight, shrunk, ((0,), (1,)))
        - dot(first, small.astype(BF), ((1,), (0,)))
    )
    scale_t = lax.dynamic_slice(scale, (0, my_t * t_cols), (1, t_cols))
    shrink_t = lax.dynamic_slice(shrink, (0, my_t * t_cols), (1, t_cols))
    grad_b = first_moment * scale_t - merged_own * shrink_t
    return (row_grad, grad_a[None], grad_b[None], grad_gain)


def solution(mesh):
    in_specs = (
        P("grp", "tp"),
        P("grp", None),
        P("grp", None),
        P(),
        P("tp", "grp"),
        P("grp", "tp", None),
        P("grp", None, None),
        P("grp", None),
    )
    out_specs = (P("grp", "tp"), P("grp", "tp", None), P("grp", None, "tp"), P("grp", None))
    return jax.shard_map(
        on_device, mesh=mesh, in_specs=in_specs, out_specs=out_specs, check_vma=False
    )
```

profile of v0, /device:TPU:1, one launch (start us, length us, event | category | flops | bytes accessed | tf_op | source)
XLA Modules:
  0.0 199.2 jit_solution(3554385559575562008)
XLA Ops:
  7.2 0.7 all-gather.5.cloned.1.call-update
  7.9 1.1 reshape_squeeze.3
  9.2 0.8 broadcast_in_dim.18
  9.9 0.8 pad_maximum_fusion.1
  10.7 4.8 %all-to-all-start.1 = ((bf16[4,32,1536]{2,1,0:T(8,128)(2,1)}), bf16[4,32,1536]{2,1,0:T(8,128)(2,1)S(1)}, u32[]{:S(2)}, u32[]{:S(2)}) async-start(bf16[4,32,1536]{2,1,0:T(8,128)(2,1)} %pad_maximum_fusion.1), calls=%async_computation.1 | async-start | bytes 786432 | tf_op jit(solution)/shard_map/all_to_all | solution.py:66
  15.5 0.7 copy.21
  16.3 0.1 reduce
  16.4 0.7 multiply_subtract_fusion
  17.1 0.1 select_reduce_fusion
  17.3 1.2 convolution_convert_fusion
  18.5 1.1 reshape.168
  19.5 2.3 %all-to-all-done.1 = bf16[4,32,1536]{2,1,0:T(8,128)(2,1)S(1)} async-done(((bf16[4,32,1536]{2,1,0:T(8,128)(2,1)}), bf16[4,32,1536]{2,1,0:T(8,128)(2,1)S(1)}, u32[]{:S(2)}, u32[]{:S(2)}) %all-to-all-start.1) | async-done | bytes 393248 | tf_op jit(solution)/shard_map/all_to_all | solution.py:66
  21.8 11.7 %all-to-all-start = ((bf16[32,12,768]{2,1,0:T(8,128)(2,1)}), bf16[32,12,768]{2,1,0:T(8,128)(2,1)S(1)}, u32[]{:S(2)}, u32[]{:S(2)}) async-start(bf16[32,12,768]{2,1,0:T(8,128)(2,1)} %reshape.168), calls=%async_computation | async-start | bytes 1572864 | tf_op jit(solution)/shard_map/all_to_all | solution.py:52
  33.5 0.2 convolution_select_fusion
  33.7 26.8 %all-to-all-done = bf16[32,12,768]{2,1,0:T(8,128)(2,1)S(1)} async-done(((bf16[32,12,768]{2,1,0:T(8,128)(2,1)}), bf16[32,12,768]{2,1,0:T(8,128)(2,1)S(1)}, u32[]{:S(2)}, u32[]{:S(2)}) %all-to-all-start) | async-done | bytes 589856 | tf_op jit(solution)/shard_map/all_to_all | solution.py:52
  60.5 0.1 reshape.169
  60.6 0.7 slice.178
  61.4 0.2 fusion.17
  61.7 4.3 %all-gather.5.cloned.1.call-done = bf16[1024,512]{0,1:T(8,128)(2,1)} async-done(((bf16[128,512]{0,1:T(8,128)(2,1)}), bf16[1024,512]{0,1:T(8,128)(2,1)}) %all-gather.5.cloned.1.call-update) | async-done | bytes 1048592 | tf_op jit(solution)/shard_map/all_gather | solution.py:47
  65.9 1.6 fusion.38
  67.6 0.5 bitcast_reduce_fusion
  68.1 0.2 reshape.171
  68.4 0.2 multiply_reduce_fusion
  68.7 0.3 concatenate.27
  68.9 5.3 %collective-permute-start = (bf16[1024,512]{0,1:T(8,128)(2,1)S(1)}, bf16[1024,512]{0,1:T(8,128)(2,1)}, u32[]{:S(2)}, u32[]{:S(2)}) collective-permute-start(bf16[1024,512]{0,1:T(8,128)(2,1)S(1)} %copy-done.1), channel_id=1, source_target_pairs={{128,0},{144,16},{160,32},{176,48},{192,64},{208,80},{224,96},{240... | collective-permute-start | bytes 3145736 | tf_op jit(solution)/shard_map/ppermute | solution.py:137
  74.2 1.9 collective-permute-start.2
  76.2 0.1 broadcast_in_dim.20
  76.3 1.0 pad_maximum_fusion
  77.3 8.9 %all-to-all-start.2 = ((bf16[16,224,128]{2,1,0:T(8,128)(2,1)}), bf16[16,224,128]{2,1,0:T(8,128)(2,1)S(1)}, u32[]{:S(2)}, u32[]{:S(2)}) async-start(bf16[16,224,128]{2,1,0:T(8,128)(2,1)} %pad_maximum_fusion), calls=%async_computation.2 | async-start | bytes 1835008 | tf_op jit(solution)/shard_map/all_to_all | solution.py:97
  86.2 8.4 %collective-permute-done = bf16[1024,512]{0,1:T(8,128)(2,1)} collective-permute-done((bf16[1024,512]{0,1:T(8,128)(2,1)S(1)}, bf16[1024,512]{0,1:T(8,128)(2,1)}, u32[]{:S(2)}, u32[]{:S(2)}) %collective-permute-start) | collective-permute-done | bytes 1048608 | tf_op jit(solution)/shard_map/ppermute | solution.py:137
  94.6 1.9 slice.213
  96.5 5.4 %collective-permute-start.1 = (bf16[512,512]{0,1:T(8,128)(2,1)}, bf16[512,512]{0,1:T(8,128)(2,1)S(1)}, u32[]{:S(2)}, u32[]{:S(2)}) collective-permute-start(bf16[512,512]{0,1:T(8,128)(2,1)} %slice.213), channel_id=1, source_target_pairs={{128,0},{144,16},{160,32},{176,48},{192,64},{208,80},{224,96},{240... | collective-permute-start | bytes 1572872 | tf_op jit(solution)/shard_map/ppermute | solution.py:137
  101.9 1.9 slice.214
  103.8 1.9 collective-permute-start.3
  105.8 2.5 %broadcast_in_dim.21 = bf16[4096,512]{0,1:T(8,128)(2,1)} broadcast(bf16[]{:T(256)} %constant.83.clone.1), dimensions={} | broadcast | bytes 4194306 | tf_op jit(solution)/shard_map/broadcast_in_dim | solution.py:143
  108.3 1.1 constant_dynamic-update-slice_fusion.10
  109.4 2.4 %constant_dynamic-update-slice_fusion.9 = bf16[4096,512]{0,1:T(8,128)(2,1)} fusion(bf16[4096,512]{0,1:T(8,128)(2,1)} %constant_dynamic-update-slice_fusion.10, bf16[1024,512]{0,1:T(8,128)(2,1)} %collective-permute-done, s32[]{:T(128)S(6)} %select_n.67), kind=kLoop, calls=%fused_computation.87 | loop fusion | bytes 2097156 | tf_op jit(solution)/shard_map/dynamic_update_slice | solution.py:145
  111.8 5.7 %collective-permute-done.3 = bf16[512,512]{0,1:T(8,128)(2,1)} collective-permute-done((bf16[512,512]{0,1:T(8,128)(2,1)}, bf16[512,512]{0,1:T(8,128)(2,1)}, u32[]{:S(2)}, u32[]{:S(2)}) %collective-permute-start.3) | collective-permute-done | bytes 524320 | tf_op jit(solution)/shard_map/ppermute | solution.py:137
  117.4 2.3 %maximum_dynamic-update-slice_fusion = bf16[4096,512]{0,1:T(8,128)(2,1)} fusion(bf16[4096,512]{0,1:T(8,128)(2,1)} %constant_dynamic-update-slice_fusion.9, s32[]{:T(128)S(6)} %select_n.69, bf16[512,512]{0,1:T(8,128)(2,1)} %collective-permute-done.3, bf16[512,512]{0,1:T(8,128)(2,1)S(1)} %collective-permute-done.1), kind=kLoop, calls=%fused_computation.21 | loop fusion | flops 2097152 | bytes 2097156 | tf_op jit(solution)/shard_map/dynamic_update_slice | solution.py:145
  119.7 2.3 %constant_dynamic-update-slice_fusion.8 = bf16[4096,512]{0,1:T(8,128)(2,1)} fusion(bf16[4096,512]{0,1:T(8,128)(2,1)} %maximum_dynamic-update-slice_fusion, bf16[1024,512]{0,1:T(8,128)(2,1)} %collective-permute-done.2, s32[]{:T(128)S(6)} %select_n.71), kind=kLoop, calls=%fused_computation.86 | loop fusion | bytes 2097156 | tf_op jit(solution)/shard_map/dynamic_update_slice | solution.py:145
  122.0 0.1 convert_reduce_fusion
  122.3 0.6 copy.24
  122.9 3.3 %all-to-all-start.3 = ((f32[4,1,1024]{2,1,0:T(1,128)}), f32[4,1,1024]{2,1,0:T(1,128)S(1)}, u32[]{:S(2)}, u32[]{:S(2)}) async-start(f32[4,1,1024]{2,1,0:T(1,128)} %copy.24), calls=%async_computation.3 | async-start | bytes 32768 | tf_op jit(solution)/shard_map/all_to_all | solution.py:112
  126.2 0.2 fusion.42
  126.4 5.4 %all-gather.3.cloned.1.call-done = bf16[384,4096]{1,0:T(8,128)(2,1)} async-done(((bf16[384,256]{1,0:T(8,128)(2,1)}), bf16[384,4096]{1,0:T(8,128)(2,1)}) %all-gather.3.cloned.1.call-update) | async-done | bytes 3145744 | tf_op jit(solution)/shard_map/all_gather | solution.py:56
  131.7 5.0 %fusion.1 = f32[4096]{0:T(1024)S(1)} fusion(bf16[384,4096]{1,0:T(8,128)(2,1)} %all-gather.3.cloned.1.call-done, bf16[4096,512]{0,1:T(8,128)(2,1)} %constant_dynamic-update-slice_fusion.8, bf16[384,768]{1,0:T(8,128)(2,1)S(1)} %copy-done.4), kind=kOutput, calls=%fused_computation.3 | convolution fusion | flops 1615327232 | bytes 7749632 | tf_op jit(solution)/shard_map/dot_general | solution.py:15
  136.7 0.2 add_dynamic-update-slice_fusion
  136.9 0.7 broadcast_in_dim.23
  137.6 4.6 %all-to-all-start.5 = ((f32[16,32,128]{2,1,0:T(8,128)}), f32[16,32,128]{2,1,0:T(8,128)S(1)}, u32[]{:S(2)}, u32[]{:S(2)}) async-start(f32[16,32,128]{2,1,0:T(8,128)} %broadcast_in_dim.23), calls=%async_computation.5 | async-start | bytes 524288 | tf_op jit(solution)/shard_map/all_to_all | solution.py:160
  142.3 0.7 collective-permute-start.4
  143.0 11.0 %all-to-all-done.5 = f32[16,32,128]{2,1,0:T(8,128)S(1)} async-done(((f32[16,32,128]{2,1,0:T(8,128)}), f32[16,32,128]{2,1,0:T(8,128)S(1)}, u32[]{:S(2)}, u32[]{:S(2)}) %all-to-all-start.5) | async-done | bytes 262176 | tf_op jit(solution)/shard_map/all_to_all | solution.py:160
  154.0 0.6 fusion.62
  154.7 3.2 %fusion.14 = bf16[384,32]{0,1:T(8,128)(2,1)S(1)} fusion(bf16[384,4096]{1,0:T(8,128)(2,1)} %all-gather.3.cloned.1.call-done, f32[4096]{0:T(1024)S(1)} %bitcast.82, bf16[1,32,4096]{2,1,0:T(8,128)(2,1)S(1)} %copy-done.2), kind=kOutput, calls=%fused_computation.17 | convolution fusion | flops 105394176 | bytes 3448832 | tf_op jit(solution)/shard_map/dot_general | solution.py:15
  157.9 0.2 fusion.19
  158.1 0.3 fusion.43
  158.4 4.0 %fusion.9 = bf16[384,512]{1,0:T(8,128)(2,1)S(1)} fusion(f32[384,512]{1,0:T(8,128)S(1)} %fusion.43, bf16[4096,512]{0,1:T(8,128)(2,1)} %constant_dynamic-update-slice_fusion.8, bf16[384,4096]{1,0:T(8,128)(2,1)S(1)} %copy-done.8, f32[4096]{0:T(1024)S(1)} %bitcast.83), kind=kOutput, calls=%fused_computation.10 | convolution fusion | flops 1615724544 | bytes 8536064 | tf_op jit(solution)/shard_map/dot_general | solution.py:15
  162.4 0.9 reshape.175
  163.3 11.1 %all-to-all-start.4 = ((bf16[32,12,512]{2,1,0:T(8,128)(2,1)}), bf16[32,12,512]{2,1,0:T(8,128)(2,1)S(1)}, u32[]{:S(2)}, u32[]{:S(2)}) async-start(bf16[32,12,512]{2,1,0:T(8,128)(2,1)} %reshape.175), calls=%async_computation.4 | async-start | bytes 1048576 | tf_op jit(solution)/shard_map/all_to_all | solution.py:149
  174.4 3.5 %convolution_subtract_fusion = f32[512,32]{0,1:T(8,128)S(1)} fusion(f32[512,32]{0,1:T(8,128)S(1)} %fusion.19, bf16[4096,512]{0,1:T(8,128)(2,1)} %constant_dynamic-update-slice_fusion.8, bf16[1,32,4096]{2,1,0:T(8,128)(2,1)S(1)} %copy-done.2, f32[4096]{0:T(1024)S(1)} %bitcast.75), kind=kOutput, calls=%fused_computation.16 | convolution fusion | flops 134627328 | bytes 4603904 | tf_op jit(solution)/shard_map/dot_general | solution.py:15
  178.0 1.0 fusion.13
  178.9 0.6 subtract_bitcast_fusion
  179.6 11.8 %all-to-all-done.4 = bf16[32,12,512]{2,1,0:T(8,128)(2,1)S(1)} async-done(((bf16[32,12,512]{2,1,0:T(8,128)(2,1)}), bf16[32,12,512]{2,1,0:T(8,128)(2,1)S(1)}, u32[]{:S(2)}, u32[]{:S(2)}) %all-to-all-start.4) | async-done | bytes 393248 | tf_op jit(solution)/shard_map/all_to_all | solution.py:149
  191.3 0.1 reshape.176
  191.4 0.9 convolution_convert_fusion.1
  (53 shorter events, 0.7 us)
Async XLA Ops:
  7.2 10.1 %copy-start = (bf16[128,4096]{1,0:T(8,128)(2,1)S(1)}, bf16[128,4096]{1,0:T(8,128)(2,1)}, u32[]{:S(2)}) copy-start(bf16[128,4096]{1,0:T(8,128)(2,1)} %param.9) | copy-start | bytes 3145732
  7.2 58.8 %all-gather.5.cloned.1.call-start = ((), (), s32[]{:S(2)}) async-start(), calls=%async_computation.7 | async-start | bytes 1179648 | tf_op jit(solution)/shard_map/all_gather | solution.py:47
  9.1 52.3 %copy-start.5 = (bf16[1,512,32]{1,2,0:T(8,128)(2,1)S(1)}, bf16[1,512,32]{1,2,0:T(8,128)(2,1)}, u32[]{:S(2)}) copy-start(bf16[1,512,32]{1,2,0:T(8,128)(2,1)} %param.13) | copy-start | bytes 98308
  10.7 11.1 %all-to-all-start.1 = ((bf16[4,32,1536]{2,1,0:T(8,128)(2,1)}), bf16[4,32,1536]{2,1,0:T(8,128)(2,1)S(1)}, u32[]{:S(2)}, u32[]{:S(2)}) async-start(bf16[4,32,1536]{2,1,0:T(8,128)(2,1)} %pad_maximum_fusion.1), calls=%async_computation.1 | async-start | bytes 786432 | tf_op jit(solution)/shard_map/all_to_all | solution.py:66
  21.8 38.7 %all-to-all-start = ((bf16[32,12,768]{2,1,0:T(8,128)(2,1)}), bf16[32,12,768]{2,1,0:T(8,128)(2,1)S(1)}, u32[]{:S(2)}, u32[]{:S(2)}) async-start(bf16[32,12,768]{2,1,0:T(8,128)(2,1)} %reshape.168), calls=%async_computation | async-start | bytes 1572864 | tf_op jit(solution)/shard_map/all_to_all | solution.py:52
  33.5 98.2 %all-gather.3.cloned.1.call-start = ((), (), s32[]{:S(2)}) async-start(), calls=%async_computation.6 | async-start | bytes 3342336 | tf_op jit(solution)/shard_map/all_gather | solution.py:56
  60.6 1.1 copy-start.3
  65.9 2.4 %copy-start.1 = (bf16[1024,512]{0,1:T(8,128)(2,1)S(1)}, bf16[1024,512]{0,1:T(8,128)(2,1)}, u32[]{:S(2)}) copy-start(bf16[1024,512]{0,1:T(8,128)(2,1)} %all-gather.5.cloned.1.call-done) | copy-start | bytes 3145732
  68.9 25.7 %collective-permute-start = (bf16[1024,512]{0,1:T(8,128)(2,1)S(1)}, bf16[1024,512]{0,1:T(8,128)(2,1)}, u32[]{:S(2)}, u32[]{:S(2)}) collective-permute-start(bf16[1024,512]{0,1:T(8,128)(2,1)S(1)} %copy-done.1), channel_id=1, source_target_pairs={{128,0},{144,16},{160,32},{176,48},{192,64},{208,80},{224,96},{240... | collective-permute-start | bytes 3145736 | tf_op jit(solution)/shard_map/ppermute | solution.py:137
  74.2 27.7 %collective-permute-start.2 = (bf16[1024,512]{0,1:T(8,128)(2,1)S(1)}, bf16[1024,512]{0,1:T(8,128)(2,1)}, u32[]{:S(2)}, u32[]{:S(2)}) collective-permute-start(bf16[1024,512]{0,1:T(8,128)(2,1)S(1)} %copy-done.1), channel_id=1, source_target_pairs={{384,0},{400,16},{416,32},{432,48},{448,64},{464,80},{480,96},{496... | collective-permute-start | bytes 3145736 | tf_op jit(solution)/shard_map/ppermute | solution.py:137
  77.3 44.7 %all-to-all-start.2 = ((bf16[16,224,128]{2,1,0:T(8,128)(2,1)}), bf16[16,224,128]{2,1,0:T(8,128)(2,1)S(1)}, u32[]{:S(2)}, u32[]{:S(2)}) async-start(bf16[16,224,128]{2,1,0:T(8,128)(2,1)} %pad_maximum_fusion), calls=%async_computation.2 | async-start | bytes 1835008 | tf_op jit(solution)/shard_map/all_to_all | solution.py:97
  96.5 15.3 %collective-permute-start.1 = (bf16[512,512]{0,1:T(8,128)(2,1)}, bf16[512,512]{0,1:T(8,128)(2,1)S(1)}, u32[]{:S(2)}, u32[]{:S(2)}) collective-permute-start(bf16[512,512]{0,1:T(8,128)(2,1)} %slice.213), channel_id=1, source_target_pairs={{128,0},{144,16},{160,32},{176,48},{192,64},{208,80},{224,96},{240... | collective-permute-start | bytes 1572872 | tf_op jit(solution)/shard_map/ppermute | solution.py:137
  103.8 13.6 %collective-permute-start.3 = (bf16[512,512]{0,1:T(8,128)(2,1)}, bf16[512,512]{0,1:T(8,128)(2,1)}, u32[]{:S(2)}, u32[]{:S(2)}) collective-permute-start(bf16[512,512]{0,1:T(8,128)(2,1)} %slice.214), channel_id=1, source_target_pairs={{384,0},{400,16},{416,32},{432,48},{448,64},{464,80},{480,96},{496... | collective-permute-start | bytes 1572872 | tf_op jit(solution)/shard_map/ppermute | solution.py:137
  109.4 16.8 %copy-start.2 = (bf16[1,32,4096]{2,1,0:T(8,128)(2,1)S(1)}, bf16[1,32,4096]{2,1,0:T(8,128)(2,1)}, u32[]{:S(2)}) copy-start(bf16[1,32,4096]{2,1,0:T(8,128)(2,1)} %param.14) | copy-start | bytes 786436
  109.4 16.8 %copy-start.4 = (bf16[384,768]{1,0:T(8,128)(2,1)S(1)}, bf16[384,768]{1,0:T(8,128)(2,1)}, u32[]{:S(2)}) copy-start(bf16[384,768]{1,0:T(8,128)(2,1)} %copy-done.3) | copy-start | bytes 1769476
  122.9 14.0 %all-to-all-start.3 = ((f32[4,1,1024]{2,1,0:T(1,128)}), f32[4,1,1024]{2,1,0:T(1,128)S(1)}, u32[]{:S(2)}, u32[]{:S(2)}) async-start(f32[4,1,1024]{2,1,0:T(1,128)} %copy.24), calls=%async_computation.3 | async-start | bytes 32768 | tf_op jit(solution)/shard_map/all_to_all | solution.py:112
  126.3 27.7 %copy-start.7 = (f32[1,4096]{1,0:T(1,128)S(1)}, f32[1,4096]{1,0:T(1,128)}, u32[]{:S(2)}) copy-start(f32[1,4096]{1,0:T(1,128)} %param.15) | copy-start | bytes 49156
  136.7 21.3 %copy-start.6 = (bf16[1,512,32]{1,2,0:T(8,128)(2,1)S(1)}, bf16[1,512,32]{1,2,0:T(8,128)(2,1)}, u32[]{:S(2)}) copy-start(bf16[1,512,32]{1,2,0:T(8,128)(2,1)} %param.13) | copy-start | bytes 98308
  137.6 16.3 %all-to-all-start.5 = ((f32[16,32,128]{2,1,0:T(8,128)}), f32[16,32,128]{2,1,0:T(8,128)S(1)}, u32[]{:S(2)}, u32[]{:S(2)}) async-start(f32[16,32,128]{2,1,0:T(8,128)} %broadcast_in_dim.23), calls=%async_computation.5 | async-start | bytes 524288 | tf_op jit(solution)/shard_map/all_to_all | solution.py:160
  142.3 36.7 %collective-permute-start.4 = (f32[32,256]{1,0:T(8,128)S(1)}, f32[32,256]{1,0:T(8,128)S(1)}, u32[]{:S(2)}, u32[]{:S(2)}) collective-permute-start(f32[32,256]{1,0:T(8,128)S(1)} %pad_maximum_fusion.2), channel_id=1, source_target_pairs={{0,0},{1,1},{2,2},{3,3},{4,128},{5,129},{6,130},{7,131},{8,256},{9... | collective-permute-start | bytes 98312 | tf_op jit(solution)/shard_map/ppermute | solution.py:131
  154.0 4.4 %copy-start.8 = (bf16[384,4096]{1,0:T(8,128)(2,1)S(1)}, bf16[384,4096]{1,0:T(8,128)(2,1)}, u32[]{:S(2)}) copy-start(bf16[384,4096]{1,0:T(8,128)(2,1)} %all-gather.3.cloned.1.call-done) | copy-start | bytes 9437188
  163.3 28.0 %all-to-all-start.4 = ((bf16[32,12,512]{2,1,0:T(8,128)(2,1)}), bf16[32,12,512]{2,1,0:T(8,128)(2,1)S(1)}, u32[]{:S(2)}, u32[]{:S(2)}) async-start(bf16[32,12,512]{2,1,0:T(8,128)(2,1)} %reshape.175), calls=%async_computation.4 | async-start | bytes 1048576 | tf_op jit(solution)/shard_map/all_to_all | solution.py:149
Sparse Core Ops, SparseCore 0:
  10.0 55.8 all-gather.4
  68.0 63.6 all-gather.2
where the time goes:
time: 200 us; the launch traced here: 199 us
  waiting for transfers between devices  76.2 us (38%)
  starting transfers between devices  59.7 us (30%)
  matrix products  22 us (11%)
  local copies, waits for them, and re-layouts  19.8 us (10%)
  between operations  14.6 us (7%)
  other arithmetic  6.93 us (3%)
    all_to_all x1, waiting for transfers between devices, on_device(): lax.all_to_all(both.reshape(groups, CAP, width + t_cols), 'grp', split_ax...  26.8 us
    dot_general x14, matrix products, dot(): lax.dot_general(left, right, (dims, ((), ())), precision=precision, prefe...  22 us
    ppermute x4, starting transfers between devices, along_x(): return lax.ppermute(values, 'grp', pairs)  14.5 us
    ppermute x4, waiting for transfers between devices, along_x(): return lax.ppermute(values, 'grp', pairs)  14.1 us
    all_to_all x1, waiting for transfers between devices, on_device(): lax.all_to_all(back.astype(BF).reshape(groups, CAP, width), 'grp', split_...  11.8 us
    all_to_all x1, starting transfers between devices, on_device(): lax.all_to_all(both.reshape(groups, CAP, width + t_cols), 'grp', split_ax...  11.7 us
    all_to_all x1, starting transfers between devices, on_device(): lax.all_to_all(back.astype(BF).reshape(groups, CAP, width), 'grp', split_...  11.1 us
    all_to_all x1, waiting for transfers between devices, on_device(): lax.all_to_all(jnp.broadcast_to(align.reshape(1, -1, 128), (shards, out_w...  11 us
  transfers between devices with their start and end apart: 13, of which 8 were waited for; matrix products, arithmetic and copies ran while one was open for 24% of the time, Pallas kernels for 0%

commit v1 on v0

--- a/solution.py
+++ b/solution.py
@@ -53,7 +53,9 @@
         both.reshape(groups, CAP, width + t_cols), "grp", split_axis=0, concat_axis=0, tiled=True
     ).reshape(packed, width + t_cols)
     rows_in, rows_grad_t = (both[:, :width], both[:, width:])
-    rows_grad = lax.all_gather(rows_grad_t, "tp", axis=1, tiled=True)
+    rows_grad = jnp.concatenate(
+        lax.all_to_all(jnp.stack([rows_grad_t] * lax.axis_size("tp")), "tp", 0, 0), axis=1
+    )
     first, second = (adapter_a[0], adapter_b[0])
     first_t = first.T
     fields = jnp.concatenate(

time: 200 us -> 276 us (1.38)
  waiting for transfers between devices: 76.2 us -> 125 us
  other arithmetic: 6.93 us -> 19.7 us
  local copies, waits for them, and re-layouts: 19.8 us -> 30.2 us
  starting transfers between devices: 59.7 us -> 63.5 us
    all_to_all x1, waiting for transfers between devices: 0.01 us -> 25.4 us  [on_device(): sums = lax.all_to_all(sums, 'tp', split_axis=0, concat_axis=0, tiled=True)]
    all_to_all x0 -> x1, waiting for transfers between devices: none -> 16.3 us  [on_device(): lax.all_to_all(jnp.stack([rows_grad_t] * lax.axis_size('tp')), 'tp', 0, 0)]
    ppermute x4, waiting for transfers between devices: 14.1 us -> 28.1 us  [along_x(): return lax.ppermute(values, 'grp', pairs)]
    convert_element_type x0 -> x2, other arithmetic: none -> 7.56 us  [on_device(): hidden = (rows_grad.astype(F32) * scale).astype(BF)]
    convert_element_type x0 -> x1, local copies, waits for them, and re-layouts: none -> 6.56 us  [on_device(): hidden = (rows_grad.astype(F32) * scale).astype(BF)]
    all_gather x1 -> x0, waiting for transfers between devices: 5.35 us -> none  [on_device(): rows_grad = lax.all_gather(rows_grad_t, 'tp', axis=1, tiled=True)]
    all_to_all x0 -> x1, local copies, waits for them, and re-layouts: none -> 4.65 us  [on_device(): lax.all_to_all(jnp.stack([rows_grad_t] * lax.axis_size('tp')), 'tp', 0, 0)]
    all_to_all x0 -> x1, starting transfers between devices: none -> 4.37 us  [on_device(): lax.all_to_all(jnp.stack([rows_grad_t] * lax.axis_size('tp')), 'tp', 0, 0)]
  transfers between devices with their start and end apart: 13 -> 13, of which waited for: 8 -> 10; matrix products, arithmetic and copies ran while one was open for 24% -> 23% of each run, Pallas kernels for 0% -> 0%
where the time goes in v1:
time: 276 us; the launch traced here: 274 us
  waiting for transfers between devices  125 us (45%)
  starting transfers between devices  63.5 us (23%)
  local copies, waits for them, and re-layouts  30.2 us (11%)
  matrix products  21 us (8%)
  other arithmetic  19.7 us (7%)
  between operations  14.6 us (5%)
    ppermute x4, waiting for transfers between devices, along_x(): return lax.ppermute(values, 'grp', pairs)  28.1 us
    all_to_all x1, waiting for transfers between devices, on_device(): lax.all_to_all(both.reshape(groups, CAP, width + t_cols), 'grp', split_ax...  26.6 us
    all_to_all x1, waiting for transfers between devices, on_device(): sums = lax.all_to_all(sums, 'tp', split_axis=0, concat_axis=0, tiled=True)  25.4 us
    dot_general x14, matrix products, dot(): lax.dot_general(left, right, (dims, ((), ())), precision=precision, prefe...  21 us
    all_to_all x1, waiting for transfers between devices, on_device(): lax.all_to_all(jnp.stack([rows_grad_t] * lax.axis_size('tp')), 'tp', 0, 0)  16.3 us
    ppermute x4, starting transfers between devices, along_x(): return lax.ppermute(values, 'grp', pairs)  13 us
    all_to_all x1, starting transfers between devices, on_device(): lax.all_to_all(both.reshape(groups, CAP, width + t_cols), 'grp', split_ax...  11.7 us
    all_to_all x1, waiting for transfers between devices, on_device(): lax.all_to_all(back.astype(BF).reshape(groups, CAP, width), 'grp', split_...  11.2 us
  transfers between devices with their start and end apart: 13, of which 10 were waited for; matrix products, arithmetic and copies ran while one was open for 23% of the time, Pallas kernels for 0%

profile of v1, /device:TPU:1, one launch (start us, length us, event | category | flops | bytes accessed | tf_op | source)
XLA Modules:
  0.0 274.3 jit_solution(12453741718198058249)
XLA Ops:
  7.2 0.7 all-gather.2.cloned.1.call-update
  7.9 1.1 reshape_squeeze.3
  9.2 0.8 broadcast_in_dim.18
  9.9 0.8 pad_maximum_fusion.1
  10.7 4.8 %all-to-all-start.2 = ((bf16[4,32,1536]{2,1,0:T(8,128)(2,1)}), bf16[4,32,1536]{2,1,0:T(8,128)(2,1)S(1)}, u32[]{:S(2)}, u32[]{:S(2)}) async-start(bf16[4,32,1536]{2,1,0:T(8,128)(2,1)} %pad_maximum_fusion.1), calls=%async_computation.2 | async-start | bytes 786432 | tf_op jit(solution)/shard_map/all_to_all | solution.py:68
  15.5 0.7 copy.28
  16.4 0.7 multiply_subtract_fusion
  17.3 1.2 convolution_convert_fusion
  18.5 1.0 reshape.180
  19.5 2.3 all-to-all-done.2
  21.8 11.7 %all-to-all-start = ((bf16[32,12,768]{2,1,0:T(8,128)(2,1)}), bf16[32,12,768]{2,1,0:T(8,128)(2,1)S(1)}, u32[]{:S(2)}, u32[]{:S(2)}) async-start(bf16[32,12,768]{2,1,0:T(8,128)(2,1)} %reshape.180), calls=%async_computation | async-start | bytes 1572864 | tf_op jit(solution)/shard_map/all_to_all | solution.py:52
  33.7 26.6 %all-to-all-done = bf16[32,12,768]{2,1,0:T(8,128)(2,1)S(1)} async-done(((bf16[32,12,768]{2,1,0:T(8,128)(2,1)}), bf16[32,12,768]{2,1,0:T(8,128)(2,1)S(1)}, u32[]{:S(2)}, u32[]{:S(2)}) %all-to-all-start) | async-done | bytes 589856 | tf_op jit(solution)/shard_map/all_to_all | solution.py:52
  60.7 5.6 %all-gather.2.cloned.1.call-done = bf16[1024,512]{0,1:T(8,128)(2,1)} async-done(((bf16[128,512]{0,1:T(8,128)(2,1)}), bf16[1024,512]{0,1:T(8,128)(2,1)}) %all-gather.2.cloned.1.call-update) | async-done | bytes 1048592 | tf_op jit(solution)/shard_map/all_gather | solution.py:47
  66.4 1.6 fusion.27
  68.0 0.5 bitcast_reduce_fusion
  69.1 0.3 concatenate.27
  69.5 1.0 pad_maximum_fusion
  70.5 9.2 %all-to-all-start.3 = ((bf16[16,224,128]{2,1,0:T(8,128)(2,1)}), bf16[16,224,128]{2,1,0:T(8,128)(2,1)}, u32[]{:S(2)}, u32[]{:S(2)}) async-start(bf16[16,224,128]{2,1,0:T(8,128)(2,1)} %pad_maximum_fusion), calls=%async_computation.3 | async-start | bytes 1835008 | tf_op jit(solution)/shard_map/all_to_all | solution.py:99
  79.7 25.4 %all-to-all-done.3 = bf16[16,224,128]{2,1,0:T(8,128)(2,1)} async-done(((bf16[16,224,128]{2,1,0:T(8,128)(2,1)}), bf16[16,224,128]{2,1,0:T(8,128)(2,1)}, u32[]{:S(2)}, u32[]{:S(2)}) %all-to-all-start.3) | async-done | bytes 917536 | tf_op jit(solution)/shard_map/all_to_all | solution.py:99
  105.1 2.0 stack.2
  107.1 4.4 %all-to-all-start.1 = ((bf16[16,384,256]{2,1,0:T(8,128)(2,1)}), bf16[16,384,256]{2,1,0:T(8,128)(2,1)}, u32[]{:S(2)}, u32[]{:S(2)}) async-start(bf16[16,384,256]{2,1,0:T(8,128)(2,1)} %stack.2), calls=%async_computation.1 | async-start | bytes 6291456 | tf_op jit(solution)/shard_map/all_to_all | solution.py:57
  111.5 3.1 %collective-permute-start.2 = (bf16[1024,512]{0,1:T(8,128)(2,1)S(1)}, bf16[1024,512]{0,1:T(8,128)(2,1)S(1)}, u32[]{:S(2)}, u32[]{:S(2)}) collective-permute-start(bf16[1024,512]{0,1:T(8,128)(2,1)S(1)} %copy-done.1), channel_id=1, source_target_pairs={{384,0},{400,16},{416,32},{432,48},{448,64},{464,80},{480,96},{496... | collective-permute-start | bytes 3145736 | tf_op jit(solution)/shard_map/ppermute | solution.py:139
  114.6 3.4 %collective-permute-start = (bf16[1024,512]{0,1:T(8,128)(2,1)S(1)}, bf16[1024,512]{0,1:T(8,128)(2,1)S(1)}, u32[]{:S(2)}, u32[]{:S(2)}) collective-permute-start(bf16[1024,512]{0,1:T(8,128)(2,1)S(1)} %copy-done.1), channel_id=1, source_target_pairs={{128,0},{144,16},{160,32},{176,48},{192,64},{208,80},{224,96},{240... | collective-permute-start | bytes 3145736 | tf_op jit(solution)/shard_map/ppermute | solution.py:139
  118.0 21.5 %collective-permute-done.2 = bf16[1024,512]{0,1:T(8,128)(2,1)S(1)} collective-permute-done((bf16[1024,512]{0,1:T(8,128)(2,1)S(1)}, bf16[1024,512]{0,1:T(8,128)(2,1)S(1)}, u32[]{:S(2)}, u32[]{:S(2)}) %collective-permute-start.2) | collective-permute-done | bytes 1048608 | tf_op jit(solution)/shard_map/ppermute | solution.py:139
  139.4 0.9 slice.214
  140.3 1.9 collective-permute-start.3
  142.3 0.9 slice.213
  143.1 0.3 copy-done.7
  143.5 4.6 %collective-permute-start.1 = (bf16[512,512]{0,1:T(8,128)(2,1)}, bf16[512,512]{0,1:T(8,128)(2,1)}, u32[]{:S(2)}, u32[]{:S(2)}) collective-permute-start(bf16[512,512]{0,1:T(8,128)(2,1)} %slice.213), channel_id=1, source_target_pairs={{128,0},{144,16},{160,32},{176,48},{192,64},{208,80},{224,96},{240... | collective-permute-start | bytes 1572872 | tf_op jit(solution)/shard_map/ppermute | solution.py:139
  148.2 2.5 broadcast_in_dim.21
  150.6 1.1 constant_dynamic-update-slice_fusion.10
  151.7 1.1 constant_dynamic-update-slice_fusion.9
  152.8 4.6 %collective-permute-done.3 = bf16[512,512]{0,1:T(8,128)(2,1)} collective-permute-done((bf16[512,512]{0,1:T(8,128)(2,1)}, bf16[512,512]{0,1:T(8,128)(2,1)}, u32[]{:S(2)}, u32[]{:S(2)}) %collective-permute-start.3) | collective-permute-done | bytes 524320 | tf_op jit(solution)/shard_map/ppermute | solution.py:139
  157.3 2.1 collective-permute-done.1
  159.4 2.4 maximum_dynamic-update-slice_fusion
  161.8 1.1 constant_dynamic-update-slice_fusion.8
  163.0 1.3 convert_reduce_fusion
  164.4 0.6 copy.33
  165.2 16.3 %all-to-all-done.1 = bf16[16,384,256]{2,1,0:T(8,128)(2,1)} async-done(((bf16[16,384,256]{2,1,0:T(8,128)(2,1)}), bf16[16,384,256]{2,1,0:T(8,128)(2,1)}, u32[]{:S(2)}, u32[]{:S(2)}) %all-to-all-start.1) | async-done | bytes 3145760 | tf_op jit(solution)/shard_map/all_to_all | solution.py:57
  181.5 4.0 %all-to-all-start.4 = ((f32[4,1,1024]{2,1,0:T(1,128)}), f32[4,1,1024]{2,1,0:T(1,128)S(1)}, u32[]{:S(2)}, u32[]{:S(2)}) async-start(f32[4,1,1024]{2,1,0:T(1,128)} %copy.33), calls=%async_computation.4 | async-start | bytes 32768 | tf_op jit(solution)/shard_map/all_to_all | solution.py:114
  185.5 4.6 %copy.29 = bf16[16,384,256]{1,2,0:T(8,128)(2,1)} copy(bf16[16,384,256]{2,1,0:T(8,128)(2,1)} %all-to-all-done.1) | data formatting | bytes 6291456 | tf_op jit(solution)/shard_map/all_to_all | solution.py:57
  190.1 5.2 %convert_element_type.122 = f32[16,384,256]{1,2,0:T(8,128)} convert(bf16[16,384,256]{1,2,0:T(8,128)(2,1)} %copy.29) | non-fusion elementwise | flops 1572864 | bytes 9437184 | tf_op jit(solution)/shard_map/convert_element_type | solution.py:148
  195.3 6.6 %copy.34 = f32[384,4096]{1,0:T(8,128)} copy(f32[384,4096]{0,1:T(8,128)} %bitcast.76) | data formatting | bytes 12582912 | tf_op jit(solution)/shard_map/convert_element_type | solution.py:148
  201.8 5.9 %multiply_reduce_fusion = f32[4096]{0:T(1024)S(1)} fusion(f32[384,4096]{1,0:T(8,128)} %copy.34, bf16[4096,512]{0,1:T(8,128)(2,1)} %constant_dynamic-update-slice_fusion.8, bf16[384,768]{1,0:T(8,128)(2,1)S(1)} %reshape.181), kind=kOutput, calls=%fused_computation | convolution fusion | flops 1613754368 | bytes 10895360 | tf_op jit(solution)/shard_map/dot_general | solution.py:15
  207.9 0.7 broadcast_in_dim.23
  208.6 5.7 %all-to-all-start.6 = ((f32[16,32,128]{2,1,0:T(8,128)}), f32[16,32,128]{2,1,0:T(8,128)}, u32[]{:S(2)}, u32[]{:S(2)}) async-start(f32[16,32,128]{2,1,0:T(8,128)} %broadcast_in_dim.23), calls=%async_computation.6 | async-start | bytes 524288 | tf_op jit(solution)/shard_map/all_to_all | solution.py:162
  214.4 0.6 pad_maximum_fusion.2
  215.0 2.0 collective-permute-start.4
  217.0 9.1 %all-to-all-done.6 = f32[16,32,128]{2,1,0:T(8,128)} async-done(((f32[16,32,128]{2,1,0:T(8,128)}), f32[16,32,128]{2,1,0:T(8,128)}, u32[]{:S(2)}, u32[]{:S(2)}) %all-to-all-start.6) | async-done | bytes 262176 | tf_op jit(solution)/shard_map/all_to_all | solution.py:162
  226.2 1.1 reduce_sum.69
  227.3 0.5 broadcast.107
  227.8 2.0 fusion.47
  229.9 2.4 multiply_convert_fusion
  232.3 0.5 convolution_convert_fusion.2
  233.0 0.3 fusion.32
  233.3 0.6 constant_dynamic-slice_fusion.1
  233.9 4.8 %fusion.3 = bf16[384,512]{1,0:T(8,128)(2,1)} fusion(f32[384,512]{1,0:T(8,128)S(1)} %fusion.32, bf16[4096,512]{0,1:T(8,128)(2,1)} %constant_dynamic-update-slice_fusion.8, f32[384,4096]{1,0:T(8,128)S(1)} %bitcast.78, f32[4096]{0:T(1024)S(1)} %bitcast.94), kind=kOutput, calls=%fused_computation.9 | convolution fusion | flops 1614151680 | bytes 11681792 | tf_op jit(solution)/shard_map/dot_general | solution.py:15
  238.7 1.9 reshape.187
  240.6 8.7 %all-to-all-start.5 = ((bf16[32,12,512]{2,1,0:T(8,128)(2,1)}), bf16[32,12,512]{2,1,0:T(8,128)(2,1)S(1)}, u32[]{:S(2)}, u32[]{:S(2)}) async-start(bf16[32,12,512]{2,1,0:T(8,128)(2,1)} %reshape.187), calls=%async_computation.5 | async-start | bytes 1048576 | tf_op jit(solution)/shard_map/all_to_all | solution.py:151
  249.3 3.5 %convolution_subtract_fusion = f32[512,32]{0,1:T(8,128)S(1)} fusion(f32[512,32]{0,1:T(8,128)S(1)} %fusion.8, bf16[4096,512]{0,1:T(8,128)(2,1)} %constant_dynamic-update-slice_fusion.8, bf16[1,32,4096]{2,1,0:T(8,128)(2,1)S(1)} %copy-done.2, f32[4096]{0:T(1024)S(1)} %bitcast.86), kind=kOutput, calls=%fused_computation.15 | convolution fusion | flops 134627328 | bytes 4603904 | tf_op jit(solution)/shard_map/dot_general | solution.py:15
  252.8 1.0 fusion.5
  253.8 1.4 subtract_bitcast_fusion
  255.2 11.2 %all-to-all-done.5 = bf16[32,12,512]{2,1,0:T(8,128)(2,1)S(1)} async-done(((bf16[32,12,512]{2,1,0:T(8,128)(2,1)}), bf16[32,12,512]{2,1,0:T(8,128)(2,1)S(1)}, u32[]{:S(2)}, u32[]{:S(2)}) %all-to-all-start.5) | async-done | bytes 393248 | tf_op jit(solution)/shard_map/all_to_all | solution.py:151
  266.5 0.9 convolution_convert_fusion.1
  (74 shorter events, 2.5 us)
Async XLA Ops:
  7.2 10.1 %copy-start = (bf16[128,4096]{1,0:T(8,128)(2,1)S(1)}, bf16[128,4096]{1,0:T(8,128)(2,1)}, u32[]{:S(2)}) copy-start(bf16[128,4096]{1,0:T(8,128)(2,1)} %param.9) | copy-start | bytes 3145732
  7.2 59.2 %all-gather.2.cloned.1.call-start = ((), (), s32[]{:S(2)}) async-start(), calls=%async_computation.7 | async-start | bytes 1179648 | tf_op jit(solution)/shard_map/all_gather | solution.py:47
  7.9 52.5 %copy-start.9 = (bf16[1,512,32]{1,2,0:T(8,128)(2,1)S(1)}, bf16[1,512,32]{1,2,0:T(8,128)(2,1)}, u32[]{:S(2)}) copy-start(bf16[1,512,32]{1,2,0:T(8,128)(2,1)} %param.13) | copy-start | bytes 98308
  10.7 11.1 %all-to-all-start.2 = ((bf16[4,32,1536]{2,1,0:T(8,128)(2,1)}), bf16[4,32,1536]{2,1,0:T(8,128)(2,1)S(1)}, u32[]{:S(2)}, u32[]{:S(2)}) async-start(bf16[4,32,1536]{2,1,0:T(8,128)(2,1)} %pad_maximum_fusion.1), calls=%async_computation.2 | async-start | bytes 786432 | tf_op jit(solution)/shard_map/all_to_all | solution.py:68
  17.2 43.1 %copy-start.12 = (s32[128]{0:T(128)}, s32[128]{0:T(128)S(1)}, u32[]{:S(2)}) copy-start(s32[128]{0:T(128)S(1)} %iota_add_fusion) | copy-start | bytes 1540
  21.8 38.5 %all-to-all-start = ((bf16[32,12,768]{2,1,0:T(8,128)(2,1)}), bf16[32,12,768]{2,1,0:T(8,128)(2,1)S(1)}, u32[]{:S(2)}, u32[]{:S(2)}) async-start(bf16[32,12,768]{2,1,0:T(8,128)(2,1)} %reshape.180), calls=%async_computation | async-start | bytes 1572864 | tf_op jit(solution)/shard_map/all_to_all | solution.py:52
  60.4 141.4 %copy-start.3 = (bf16[384,768]{1,0:T(8,128)(2,1)}, bf16[384,768]{1,0:T(8,128)(2,1)S(1)}, u32[]{:S(2)}) copy-start(bf16[384,768]{1,0:T(8,128)(2,1)S(1)} %reshape.181) | copy-start | bytes 1769476
  66.4 2.5 copy-start.1
  70.5 34.6 %all-to-all-start.3 = ((bf16[16,224,128]{2,1,0:T(8,128)(2,1)}), bf16[16,224,128]{2,1,0:T(8,128)(2,1)}, u32[]{:S(2)}, u32[]{:S(2)}) async-start(bf16[16,224,128]{2,1,0:T(8,128)(2,1)} %pad_maximum_fusion), calls=%async_computation.3 | async-start | bytes 1835008 | tf_op jit(solution)/shard_map/all_to_all | solution.py:99
  107.1 74.4 %all-to-all-start.1 = ((bf16[16,384,256]{2,1,0:T(8,128)(2,1)}), bf16[16,384,256]{2,1,0:T(8,128)(2,1)}, u32[]{:S(2)}, u32[]{:S(2)}) async-start(bf16[16,384,256]{2,1,0:T(8,128)(2,1)} %stack.2), calls=%async_computation.1 | async-start | bytes 6291456 | tf_op jit(solution)/shard_map/all_to_all | solution.py:57
  111.5 28.0 %collective-permute-start.2 = (bf16[1024,512]{0,1:T(8,128)(2,1)S(1)}, bf16[1024,512]{0,1:T(8,128)(2,1)S(1)}, u32[]{:S(2)}, u32[]{:S(2)}) collective-permute-start(bf16[1024,512]{0,1:T(8,128)(2,1)S(1)} %copy-done.1), channel_id=1, source_target_pairs={{384,0},{400,16},{416,32},{432,48},{448,64},{464,80},{480,96},{496... | collective-permute-start | bytes 3145736 | tf_op jit(solution)/shard_map/ppermute | solution.py:139
  114.6 27.6 %collective-permute-start = (bf16[1024,512]{0,1:T(8,128)(2,1)S(1)}, bf16[1024,512]{0,1:T(8,128)(2,1)S(1)}, u32[]{:S(2)}, u32[]{:S(2)}) collective-permute-start(bf16[1024,512]{0,1:T(8,128)(2,1)S(1)} %copy-done.1), channel_id=1, source_target_pairs={{128,0},{144,16},{160,32},{176,48},{192,64},{208,80},{224,96},{240... | collective-permute-start | bytes 3145736 | tf_op jit(solution)/shard_map/ppermute | solution.py:139
  139.4 2.8 %copy-start.5 = (bf16[1024,512]{0,1:T(8,128)(2,1)}, bf16[1024,512]{0,1:T(8,128)(2,1)S(1)}, u32[]{:S(2)}) copy-start(bf16[1024,512]{0,1:T(8,128)(2,1)S(1)} %collective-permute-done.2) | copy-start | bytes 3145732
  140.3 17.0 %collective-permute-start.3 = (bf16[512,512]{0,1:T(8,128)(2,1)}, bf16[512,512]{0,1:T(8,128)(2,1)}, u32[]{:S(2)}, u32[]{:S(2)}) collective-permute-start(bf16[512,512]{0,1:T(8,128)(2,1)} %slice.214), channel_id=1, source_target_pairs={{384,0},{400,16},{416,32},{432,48},{448,64},{464,80},{480,96},{496... | collective-permute-start | bytes 1572872 | tf_op jit(solution)/shard_map/ppermute | solution.py:139
  142.2 1.2 copy-start.7
  143.5 16.0 %collective-permute-start.1 = (bf16[512,512]{0,1:T(8,128)(2,1)}, bf16[512,512]{0,1:T(8,128)(2,1)}, u32[]{:S(2)}, u32[]{:S(2)}) collective-permute-start(bf16[512,512]{0,1:T(8,128)(2,1)} %slice.213), channel_id=1, source_target_pairs={{128,0},{144,16},{160,32},{176,48},{192,64},{208,80},{224,96},{240... | collective-permute-start | bytes 1572872 | tf_op jit(solution)/shard_map/ppermute | solution.py:139
  148.1 3.5 %copy-start.8 = (bf16[1024,512]{0,1:T(8,128)(2,1)S(1)}, bf16[1024,512]{0,1:T(8,128)(2,1)}, u32[]{:S(2)}) copy-start(bf16[1024,512]{0,1:T(8,128)(2,1)} %copy-done.7) | copy-start | bytes 3145732
  150.6 11.2 %copy-start.6 = (bf16[1024,512]{0,1:T(8,128)(2,1)S(1)}, bf16[1024,512]{0,1:T(8,128)(2,1)}, u32[]{:S(2)}) copy-start(bf16[1024,512]{0,1:T(8,128)(2,1)} %copy-done.5) | copy-start | bytes 3145732
  151.7 13.3 %copy-start.2 = (bf16[1,32,4096]{2,1,0:T(8,128)(2,1)S(1)}, bf16[1,32,4096]{2,1,0:T(8,128)(2,1)}, u32[]{:S(2)}) copy-start(bf16[1,32,4096]{2,1,0:T(8,128)(2,1)} %param.14) | copy-start | bytes 786436
  181.5 26.4 %all-to-all-start.4 = ((f32[4,1,1024]{2,1,0:T(1,128)}), f32[4,1,1024]{2,1,0:T(1,128)S(1)}, u32[]{:S(2)}, u32[]{:S(2)}) async-start(f32[4,1,1024]{2,1,0:T(1,128)} %copy.33), calls=%async_computation.4 | async-start | bytes 32768 | tf_op jit(solution)/shard_map/all_to_all | solution.py:114
  208.6 17.5 %all-to-all-start.6 = ((f32[16,32,128]{2,1,0:T(8,128)}), f32[16,32,128]{2,1,0:T(8,128)}, u32[]{:S(2)}, u32[]{:S(2)}) async-start(f32[16,32,128]{2,1,0:T(8,128)} %broadcast_in_dim.23), calls=%async_computation.6 | async-start | bytes 524288 | tf_op jit(solution)/shard_map/all_to_all | solution.py:162
  215.0 38.8 %collective-permute-start.4 = (f32[32,256]{1,0:T(8,128)}, f32[32,256]{1,0:T(8,128)}, u32[]{:S(2)}, u32[]{:S(2)}) collective-permute-start(f32[32,256]{1,0:T(8,128)} %pad_maximum_fusion.2), channel_id=1, source_target_pairs={{0,0},{1,1},{2,2},{3,3},{4,128},{5,129},{6,130},{7,131},{8,256},{9... | collective-permute-start | bytes 98312 | tf_op jit(solution)/shard_map/ppermute | solution.py:133
  226.2 7.7 %slice-start = ((s8[6291456]{0:T(1024)(128)(4,1)}), s8[2097152]{0:T(1024)(128)(4,1)S(1)}, s32[]{:S(2)}) async-start(s8[6291456]{0:T(1024)(128)(4,1)} %bitcast.77), calls=%async_computation.8 | async-start | bytes 4194304
  229.8 3.0 %copy-start.4 = (bf16[384,768]{1,0:T(8,128)(2,1)S(1)}, bf16[384,768]{1,0:T(8,128)(2,1)}, u32[]{:S(2)}) copy-start(bf16[384,768]{1,0:T(8,128)(2,1)} %copy-done.3) | copy-start | bytes 1769476
  229.8 3.5 %copy-start.10 = (f32[1,4096]{1,0:T(1,128)S(1)}, f32[1,4096]{1,0:T(1,128)}, u32[]{:S(2)}) copy-start(f32[1,4096]{1,0:T(1,128)} %get-tuple-element.5) | copy-start | bytes 49156
  229.9 4.0 %slice-start.1 = ((s8[6291456]{0:T(1024)(128)(4,1)}), s8[4194304]{0:T(1024)(128)(4,1)S(1)}, s32[]{:S(2)}) async-start(s8[6291456]{0:T(1024)(128)(4,1)} %bitcast.77), calls=%async_computation.9 | async-start | bytes 8388608
  238.7 15.1 %copy-start.11 = (f32[1,256]{1,0:T(1,128)S(1)}, f32[1,256]{1,0:T(1,128)}, u32[]{:S(2)}) copy-start(f32[1,256]{1,0:T(1,128)} %constant_dynamic-slice_fusion.1) | copy-start | bytes 3076
  238.7 27.8 %copy-start.13 = (s32[128]{0:T(128)S(1)}, s32[128]{0:T(128)}, u32[]{:S(2)}) copy-start(s32[128]{0:T(128)} %copy-done.12) | copy-start | bytes 1540
  240.6 25.8 %all-to-all-start.5 = ((bf16[32,12,512]{2,1,0:T(8,128)(2,1)}), bf16[32,12,512]{2,1,0:T(8,128)(2,1)S(1)}, u32[]{:S(2)}, u32[]{:S(2)}) async-start(bf16[32,12,512]{2,1,0:T(8,128)(2,1)} %reshape.187), calls=%async_computation.5 | async-start | bytes 1048576 | tf_op jit(solution)/shard_map/all_to_all | solution.py:151
Sparse Core Ops, SparseCore 0:
  10.0 56.2 all-gather.1
